TPU v7x, 1024 devices: a whole 8x8x8 slice. The times are simulated.
1024 devices in a mesh: dp: 64 (over y, x), expert: 16 (over z, core).
Axes of the slice: x: 8, y: 8, z: 8, core: 2. Of those that a mesh axis runs over, the one named last changes fastest.
Arguments:
- tokens: bfloat16 [131072, 1024], P(('dp', 'expert')), may hold values from -6 to 6
- expert_ids: int32 [131072, 2], P(('dp', 'expert')), may hold values from 0 to 15, all different within a row; in each aligned block of 128 rows (0 to 127, 128 to 255, ...) at most 24 rows name the same one
- routing: float32 [131072, 2], P(('dp', 'expert')), may hold values from 0.2 to 1
- w_gate: bfloat16 [16, 1024, 384], P('expert', 'dp'), may hold values from -0.1875 to 0.1875
- w_up: bfloat16 [16, 1024, 384], P('expert', 'dp'), may hold values from -0.1875 to 0.1875
- w_down: bfloat16 [16, 1024, 384], P('expert', 'dp'), may hold values from -0.3125 to 0.3125
- grad_out: bfloat16 [131072, 1024], P(('dp', 'expert')), may hold values from -6 to 6
Outputs:
- output: bfloat16 [131072, 1024], P(('dp', 'expert'))
- token_grad: bfloat16 [131072, 1024], P(('dp', 'expert'))
- down_grad: float32 [16, 1024, 384], P('expert', 'dp')
Inputs may be any that keep to these rules, and one draw needn't show every extreme that they name: `expert_ids`: the 2 experts of a token differ. Among the 128 tokens of one device no expert is named by more than 24 (token, choice) pairs, and in every draw some device names some expert exactly 24 times.
All inputs are finite; a program needn't handle non-finite values.
Results may differ from a plain program's by a relative error of at most 0.0065.
Values may be sent and summed in bfloat16 or wider, within the bound.
A program may use at most 32 MiB of HBM per device.

v0:
```python
import jax
import jax.numpy as jnp
from jax import lax
from jax.sharding import Mesh
from jax.sharding import PartitionSpec as P

DP = ("dp_0", "dp_1")
DP_EXPERT = ("dp_0", "dp_1", "expert")


contract_last = (((1,), (1,)), ((), ()))
contract_first = (((0,), (0,)), ((), ()))


def side_by_side(arrays, axis, dim, along):
    widths = [a.shape[along] for a in arrays]
    both = jnp.concatenate(arrays, axis=along)
    result = lax.all_gather(both, axis, axis=dim, tiled=True)
    return tuple(jnp.split(result, [sum(widths[:k]) for k in range(1, len(widths))], axis=along))


def in_one_piece(arrays, axis, split_dim, concat_dim, along):
    ends, at = ([], 0)
    for a in arrays[:-1]:
        at += a.shape[along]
        ends.append(at)
    both = jnp.concatenate(arrays, axis=along)
    return tuple(
        jnp.split(
            lax.all_to_all(both, axis, split_axis=split_dim, concat_axis=concat_dim, tiled=True),
            ends,
            axis=along,
        )
    )


def summed_rows(subtotal, axes):
    for axis in axes:
        subtotal = lax.psum_scatter(subtotal, axis, scatter_dimension=0, tiled=True)
    return subtotal


def forward_rows(row_data, gate_w, up_w, down_w):
    gate_pre = jnp.dot(row_data, gate_w, preferred_element_type=jnp.float32)
    up_pre = jnp.dot(row_data, up_w, preferred_element_type=jnp.float32)
    sigmoid_val = jax.nn.sigmoid(gate_pre)
    hidden = (gate_pre * sigmoid_val * up_pre).astype(jnp.bfloat16)
    expert_out = lax.dot_general(
        hidden, down_w, contract_last, preferred_element_type=jnp.float32
    ).astype(jnp.bfloat16)
    return (gate_pre, up_pre, hidden, expert_out)


def backward_rows(grad_rows, gate_pre, up_pre, gate_w, up_w, down_w):
    hidden_grad = jnp.dot(grad_rows, down_w, preferred_element_type=jnp.float32)
    sigmoid_val = jax.nn.sigmoid(gate_pre)
    slope_val = sigmoid_val * (1.0 + gate_pre * (1.0 - sigmoid_val))
    gate_grad = (hidden_grad * up_pre * slope_val).astype(jnp.bfloat16)
    up_grad = (hidden_grad * gate_pre * sigmoid_val).astype(jnp.bfloat16)
    summed = lax.dot_general(gate_grad, gate_w, contract_last, preferred_element_type=jnp.float32)
    summed = summed + lax.dot_general(
        up_grad, up_w, contract_last, preferred_element_type=jnp.float32
    )
    return summed.astype(jnp.bfloat16)


def local(tokens, expert_ids, routing, w_gate, w_up, w_down, grad_out):
    tok_rows, width = tokens.shape
    groups = lax.axis_size("expert")
    local_count = w_gate.shape[0]
    ff_width = w_gate.shape[2]
    experts_all = local_count * groups
    top_count = expert_ids.shape[1]
    capacity = 3 * tok_rows * top_count // (2 * experts_all)
    pair_count = tok_rows * top_count
    chosen = expert_ids.reshape(pair_count)
    onehot = (chosen[:, None] == jnp.arange(experts_all, dtype=jnp.int32)[None, :]).astype(
        jnp.int32
    )
    before = jnp.cumsum(onehot, axis=0) - onehot
    slot_index = jnp.sum(before * onehot, axis=1)
    flat_index = chosen * capacity + slot_index
    owner_row = jnp.arange(pair_count, dtype=jnp.int32) // top_count
    slot_owner = (
        jnp.full((experts_all * capacity,), tok_rows, jnp.int32).at[flat_index].set(owner_row)
    )
    weight_slot = (
        jnp.zeros((experts_all * capacity,), jnp.float32)
        .at[flat_index]
        .set(routing.reshape(pair_count))
    )
    zero_row = jnp.zeros((1, width), jnp.bfloat16)
    send_rows = jnp.concatenate([tokens, zero_row], axis=0)[slot_owner].reshape(
        experts_all, capacity, width
    )
    grads_picked = jnp.concatenate([grad_out, zero_row], axis=0)[slot_owner].astype(jnp.float32)
    send_grads = (
        (weight_slot[:, None] * grads_picked)
        .astype(jnp.bfloat16)
        .reshape(experts_all, capacity, width)
    )
    gate_full, up_full, down_full = side_by_side((w_gate, w_up, w_down), DP, 1, 0)
    recv_rows, recv_grads = in_one_piece((send_rows, send_grads), "expert", 0, 0, 1)
    rows_x = recv_rows.reshape(groups, local_count, capacity, width)
    rows_g = recv_grads.reshape(groups, local_count, capacity, width)
    slab_rows = groups * capacity
    expert_index = 0
    x_rows = rows_x[:, expert_index].reshape(slab_rows, width)
    g_rows = rows_g[:, expert_index].reshape(slab_rows, width)
    gate_w = gate_full[expert_index]
    up_w = up_full[expert_index]
    down_w = down_full[expert_index]
    is_valid = None
    position = None
    live_rows = None
    g_used = g_rows
    gate_pre, up_pre, hidden, expert_out = forward_rows(x_rows, gate_w, up_w, down_w)
    out_parts = [expert_out]
    forward_parts = [(gate_pre, up_pre, hidden, g_used, is_valid, position, live_rows)]
    out_send = jnp.stack(out_parts, axis=1).reshape(groups * local_count, capacity, width)
    expert_index = 0
    gate_pre, up_pre, hidden, g_used, is_valid, position, live_rows = forward_parts[expert_index]
    gate_w = gate_full[expert_index]
    up_w = up_full[expert_index]
    down_w = down_full[expert_index]
    grad_parts = [backward_rows(g_used, gate_pre, up_pre, gate_w, up_w, down_w)]
    grad_send = jnp.stack(grad_parts, axis=1).reshape(groups * local_count, capacity, width)
    back_out, back_grad = in_one_piece((out_send, grad_send), "expert", 0, 0, 1)
    out_rows = back_out.reshape(experts_all * capacity, width)[flat_index].reshape(
        tok_rows, top_count, width
    )
    output = jnp.sum(routing[:, :, None] * out_rows.astype(jnp.float32), axis=1).astype(
        jnp.bfloat16
    )
    grad_rows = back_grad.reshape(experts_all * capacity, width)[flat_index].reshape(
        tok_rows, top_count, width
    )
    token_grad = jnp.sum(grad_rows.astype(jnp.float32), axis=1).astype(jnp.bfloat16)
    shard_rows = w_gate.shape[1]
    saved = forward_parts[0]
    grad_cols = saved[3]
    pieces = lax.dot_general(
        grad_cols, saved[2], contract_first, preferred_element_type=jnp.float32
    )
    summed = summed_rows(pieces, DP)
    down_grad = jnp.transpose(
        (summed / lax.axis_size(DP)).reshape(shard_rows, local_count, ff_width), (1, 0, 2)
    )
    return (output, token_grad, down_grad)


def solution(mesh):
    finer = Mesh(mesh.devices.reshape(8, 8, mesh.shape["expert"]), ("dp_0", "dp_1", "expert"))
    return jax.shard_map(
        local,
        mesh=finer,
        in_specs=(
            P(DP_EXPERT, None),
            P(DP_EXPERT, None),
            P(DP_EXPERT, None),
            P("expert", DP, None),
            P("expert", DP, None),
            P("expert", DP, None),
            P(DP_EXPERT, None),
        ),
        out_specs=(P(DP_EXPERT, None), P(DP_EXPERT, None), P("expert", DP, None)),
        check_vma=False,
    )
```

profile of v0, /device:TPU:2, one launch (start us, length us, event | category | flops | bytes accessed | tf_op | source)
XLA Modules:
  0.0 216.2 jit_solution(826629119983808031)
XLA Ops:
  7.2 1.4 pad_maximum_fusion.2
  8.7 0.8 copy.13
  9.6 0.7 broadcast_multiply_fusion
  10.7 0.8 copy.11
  11.6 0.6 reduce-window.6
  12.5 1.4 scatter_custom_fusion.1
  14.0 1.0 concatenate.15
  15.0 1.0 concatenate.16
  16.0 1.4 scatter_custom_fusion
  17.4 2.1 gather_fusion.1
  19.5 2.1 gather_fusion
  21.9 55.1 %all_to_all.10 = bf16[16,48,1024]{2,1,0:T(8,128)(2,1)S(1)} all-to-all(bf16[16,48,1024]{2,1,0:T(8,128)(2,1)S(1)} %pad_maximum_fusion), channel_id=1, replica_groups=mesh['dp_0'=8,'dp_1'=8,'expert'=16] {'expert'}, dimensions={0} | all-to-all | bytes 3145728 | tf_op jit(solution)/shard_map/all_to_all | solution.py:30
  77.1 35.9 %all-gather.2.cloned.1.call-done = bf16[3,1024,384]{2,1,0:T(8,128)(2,1)} async-done(((bf16[3,16,384]{2,1,0:T(8,128)(2,1)}), bf16[3,1024,384]{2,1,0:T(8,128)(2,1)}) %all-gather.2.cloned.1.call-update) | async-done | bytes 2359312 | tf_op jit(solution)/shard_map/all_gather | solution.py:18
  113.0 1.7 fusion.2
  114.7 2.8 %multiply_convert_fusion.2 = (bf16[384,384]{1,0:T(8,128)(2,1)S(1)}, f32[384,384]{1,0:T(8,128)}) fusion(f32[384,384]{1,0:T(8,128)S(1)} %fusion.2, bf16[384,1024]{1,0:T(8,128)(2,1)S(1)} %bitcast.61, bf16[3,1024,384]{2,1,0:T(8,128)(2,1)} %all-gather.2.cloned.1.call-done), kind=kOutput, calls=%fused_computation.22 | convolution fusion | flops 302874624 | bytes 3047424 | tf_op jit(solution)/shard_map/dot_general | solution.py:45
  117.5 1.9 fusion.19
  119.4 0.6 fusion.4
  119.9 0.5 copy-done.2
  120.6 0.7 fusion.1
  121.3 0.6 add_convert_fusion
  121.9 0.6 convolution_convert_fusion
  122.5 1.3 pad_maximum_fusion.1
  123.8 8.2 %all-to-all-start.1 = ((bf16[16,48,1024]{2,1,0:T(8,128)(2,1)}), bf16[16,48,1024]{2,1,0:T(8,128)(2,1)S(1)}, u32[]{:S(2)}, u32[]{:S(2)}) async-start(bf16[16,48,1024]{2,1,0:T(8,128)(2,1)} %pad_maximum_fusion.1), calls=%async_computation.1 | async-start | bytes 3145728 | tf_op jit(solution)/shard_map/all_to_all | solution.py:30
  132.3 31.3 %reduce-scatter.3.cloned.1.call-done = f32[128,384]{1,0:T(8,128)} async-done(((f32[1024,384]{1,0:T(8,128)}), f32[128,384]{1,0:T(8,128)}) %reduce-scatter.3.cloned.1.call-update) | async-done | bytes 196624 | tf_op jit(solution)/shard_map/reduce_scatter | solution.py:39
  163.6 6.3 %all-to-all-done.1 = bf16[16,48,1024]{2,1,0:T(8,128)(2,1)S(1)} async-done(((bf16[16,48,1024]{2,1,0:T(8,128)(2,1)}), bf16[16,48,1024]{2,1,0:T(8,128)(2,1)S(1)}, u32[]{:S(2)}, u32[]{:S(2)}) %all-to-all-start.1) | async-done | bytes 1572896 | tf_op jit(solution)/shard_map/all_to_all | solution.py:30
  170.0 1.2 gather_fusion.3
  171.4 2.1 reduce_sum.35
  173.5 1.2 gather_fusion.2
  174.7 0.7 reshape.88
  175.3 2.1 multiply_reduce_fusion
  177.4 30.9 %reduce-scatter.5.cloned.1.call-done = f32[16,384]{1,0:T(8,128)} async-done(((f32[128,384]{1,0:T(8,128)}), f32[16,384]{1,0:T(8,128)}) %reduce-scatter.5.cloned.1.call-update) | async-done | bytes 24592 | tf_op jit(solution)/shard_map/reduce_scatter | solution.py:39
  208.3 1.3 multiply_bitcast_fusion
  (34 shorter events, 2.4 us)
Async XLA Ops:
  7.2 105.8 %all-gather.2.cloned.1.call-start = ((), (), s32[]{:S(2)}) async-start(), calls=%async_computation.4 | async-start | bytes 2396160 | tf_op jit(solution)/shard_map/all_gather | solution.py:18
  8.6 155.0 %reduce-scatter.3.cloned.1.call-start = ((), (), s32[]{:S(2)}) async-start(), calls=%async_computation.5 | async-start | bytes 1769472 | tf_op jit(solution)/shard_map/reduce_scatter | solution.py:39
  114.7 2.8 %copy-start.1 = (f32[384,384]{1,0:T(8,128)}, f32[384,384]{1,0:T(8,128)S(1)}, u32[]{:S(2)}) copy-start(f32[384,384]{1,0:T(8,128)S(1)} %fusion.2) | copy-start | bytes 1769476
  117.5 1.9 copy-start
  119.4 1.1 copy-start.2
  119.4 1.2 copy-start.3
  123.8 46.1 %all-to-all-start.1 = ((bf16[16,48,1024]{2,1,0:T(8,128)(2,1)}), bf16[16,48,1024]{2,1,0:T(8,128)(2,1)S(1)}, u32[]{:S(2)}, u32[]{:S(2)}) async-start(bf16[16,48,1024]{2,1,0:T(8,128)(2,1)} %pad_maximum_fusion.1), calls=%async_computation.1 | async-start | bytes 3145728 | tf_op jit(solution)/shard_map/all_to_all | solution.py:30
  132.0 76.2 %reduce-scatter.5.cloned.1.call-start = ((), (), s32[]{:S(2)}) async-start(), calls=%async_computation.6 | async-start | bytes 221184 | tf_op jit(solution)/shard_map/reduce_scatter | solution.py:39
Sparse Core Ops, SparseCore 0:
  12.8 100.1 all-gather.1
  119.5 44.0 reduce-scatter.2
  167.0 41.2 reduce-scatter.4
where the time goes:
time: 217 us; the launch traced here: 216 us
  waiting for transfers between devices  104 us (48%)
  blocking collectives  55.1 us (25%)
  local copies, waits for them, and re-layouts  15.5 us (7%)
  between operations  14 us (6%)
  other arithmetic  9.95 us (5%)
  matrix products  8.77 us (4%)
  starting transfers between devices  8.52 us (4%)
    reduce_scatter x2, waiting for transfers between devices, summed_rows(): subtotal = lax.psum_scatter(subtotal, axis, scatter_dimension=0, tiled=True)  62.2 us
    all_to_all x1, blocking collectives, in_one_piece(): lax.all_to_all(both, axis, split_axis=split_dim, concat_axis=concat_dim,...  55.1 us
    all_gather x1, waiting for transfers between devices, side_by_side(): result = lax.all_gather(both, axis, axis=dim, tiled=True)  35.9 us
    all_to_all x1, starting transfers between devices, in_one_piece(): lax.all_to_all(both, axis, split_axis=split_dim, concat_axis=concat_dim,...  8.22 us
    all_to_all x1, waiting for transfers between devices, in_one_piece(): lax.all_to_all(both, axis, split_axis=split_dim, concat_axis=concat_dim,...  6.27 us
  transfers between devices with their start and end apart: 4, of which 4 were waited for; matrix products, arithmetic and copies ran while one was open for 11% of the time, Pallas kernels for 0%

commit v1 on v0

v1 whole, which is shorter than its diff:
```python
import jax
import jax.numpy as jnp
from jax import lax
from jax.experimental import pallas as pl
from jax.experimental.pallas import tpu as pltpu
from jax.sharding import Mesh
from jax.sharding import PartitionSpec as P

MESH = pl.DeviceIdType.MESH
F32 = jnp.float32
BF16 = jnp.bfloat16
SIDE = 8
BLOCKS = 16
CAP = 24
PAIR = 2 * CAP
ROWS = BLOCKS * CAP
WIDTH = 1024
FF = 384
SHARD = 16
ORDER = (8, 9, 10, 11, 4, 5, 6, 7, 12, 13, 14, 15, 2, 3, 1)


def mm(a, b):
    return jnp.dot(a, b, preferred_element_type=F32)


def mm_nt(a, b):
    return lax.dot_general(a, b, (((1,), (1,)), ((), ())), preferred_element_type=F32)


def mm_tn(a, b):
    return lax.dot_general(a, b, (((0,), (0,)), ((), ())), preferred_element_type=F32)


def kernel(
    tok_ref,
    ids_ref,
    rout_ref,
    wg_ref,
    wu_ref,
    wd_ref,
    go_ref,
    out_ref,
    tg_ref,
    dg_ref,
    sh,
    wbuf,
    sendb,
    recv,
    xs,
    gs,
    outb,
    back,
    dwb,
    rs1,
    s1b,
    rs2,
    pz,
    pzr,
    gx,
    p_s,
    p_r,
    s1_s,
    s1_r,
    up_s,
    up_r,
    dn_s,
    dn_r,
    d_s,
    d_r,
    b_s,
    b_r,
    q_s,
    q_r,
    t_s,
    t_r,
    e_s,
    e_r,
):
    y, x = lax.axis_index("y"), lax.axis_index("x")
    z, c = lax.axis_index("z"), lax.axis_index("c")

    def wrap(v):
        return lax.rem(v + 2 * SIDE, SIDE)

    sign = 1 - 2 * c
    partner = {"z": wrap(z + 4)}
    mix = lax.rem(z // 4 + lax.rem(x, 2), 2)

    def steps(i, core):
        k, f = i // 4, (i // 2) % 2
        way = 1 - 2 * core
        dz = (0, 1, 2 * way, -1)[k]
        return dz, f * way, i % 2

    def target(i):
        dz, dx, m = steps(i, c)
        return {"x": wrap(x + dx), "z": wrap(z + dz), "c": lax.rem(c + m, 2)}

    def origin(i):
        m = i % 2
        core = lax.rem(c + m, 2)
        dz, dx, _ = steps(i, core)
        return {"x": wrap(x - dx), "z": wrap(z - dz), "c": core}

    def copy(src, dst, send, recv_sem, device):
        return pltpu.make_async_remote_copy(
            src_ref=src,
            dst_ref=dst,
            send_sem=send,
            recv_sem=recv_sem,
            device_id=device,
            device_id_type=MESH,
        )

    barrier = pltpu.get_barrier_semaphore()

    def greet(device):
        pl.semaphore_signal(barrier, inc=1, device_id=device, device_id_type=MESH)

    for i in range(1, BLOCKS):
        greet(target(i))
        greet(origin(i))
    for o in range(1, SIDE):
        greet({"x": wrap(x + o)})
        greet({"y": wrap(y + o)})
    greet(partner)
    sh[0, 0] = wg_ref[0]
    sh[0, 1] = wu_ref[0]
    sh[0, 2] = wd_ref[0]

    ids = ids_ref[...]
    id0, id1 = ids[:, 0:1], ids[:, 1:2]
    n_tok = ids.shape[0]
    lanes = lax.broadcasted_iota(jnp.int32, (n_tok, 128), 1)
    named = jnp.where((lanes == id0) | (lanes == id1), 1.0, 0.0).astype(BF16)
    row_i = lax.broadcasted_iota(jnp.int32, (n_tok, n_tok), 0)
    col_i = lax.broadcasted_iota(jnp.int32, (n_tok, n_tok), 1)
    lower = jnp.where(col_i < row_i, 1.0, 0.0).astype(BF16)
    before = mm(lower, named)

    def slot_of(expert):
        rank = jnp.sum(jnp.where(lanes == expert, before, 0.0), axis=1, keepdims=True)
        k = ((expert >> 1) - z + SIDE) & 3
        f = ((expert >> 3) + x) & 1
        m = (expert + c) & 1
        return (k * 4 + f * 2 + m) * PAIR + rank.astype(jnp.int32)

    slot0, slot1 = slot_of(id0), slot_of(id1)
    slots = lax.broadcasted_iota(jnp.int32, (n_tok, BLOCKS * PAIR), 1)

    def mark(slot):
        return jnp.where(slots == slot, 1.0, 0.0)

    gx[0] = mark(slot0).astype(BF16)
    gx[1] = mark(slot1).astype(BF16)
    gx[2] = mark(slot0 + CAP).astype(BF16)
    gx[3] = mark(slot1 + CAP).astype(BF16)
    rout = rout_ref[...]
    r0, r1 = rout[:, 0:1], rout[:, 1:2]
    cot = go_ref[...].astype(F32)
    staged = jnp.concatenate(
        [tok_ref[...], (r0 * cot).astype(BF16), (r1 * cot).astype(BF16)], axis=0
    )

    pl.semaphore_wait(barrier, 2 * (BLOCKS - 1) + 2 * (SIDE - 1) + 1)

    swap = copy(sh.at[0], sh.at[1], p_s, p_r, partner)
    swap.start()

    def row_copy(which, i):
        off = 2 * i + (mix if which == 0 else 1 - mix)
        dest = {"x": lax.rem(x + off, SIDE)}
        return off, copy(
            sh.at[which], wbuf.at[y, x], s1_s.at[off], s1_r.at[off], dest
        )

    def row_sends(which):
        for i in range(4):
            off, sent = row_copy(which, i)
            if i == 0:

                @pl.when(off == 0)
                def _():
                    wbuf[y, x] = sh[which]

                @pl.when(off != 0)
                def _():
                    sent.start()
            else:
                sent.start()

    row_sends(0)

    chosen = jnp.concatenate([gx[0] + gx[1], gx[2], gx[3]], axis=0)
    quarter = BLOCKS * PAIR // 4
    for part in (2, 1, 3, 0):
        cols = chosen[:, part * quarter : (part + 1) * quarter]
        packed = mm_tn(cols, staged).astype(BF16)
        sendb[pl.ds(part * quarter, quarter)] = packed
        for i in ORDER:
            if i // 4 == part:
                here = pl.ds(i * PAIR, PAIR)
                copy(
                    sendb.at[here], recv.at[here], d_s.at[i], d_r.at[i], target(i)
                ).start()
    recv[pl.ds(0, PAIR)] = sendb[pl.ds(0, PAIR)]

    swap.wait_recv()
    row_sends(1)

    above, below = {"y": wrap(y + 1)}, {"y": wrap(y - 1)}

    def place(p):
        return lax.rem(x - p + SIDE, SIDE)

    def up_copy(d, p):
        block = wbuf.at[wrap(y - d), place(p)]
        return copy(block, block, up_s.at[d, p], up_r.at[d, p], above)

    def down_copy(d, p):
        block = wbuf.at[wrap(y + d), place(p)]
        return copy(block, block, dn_s.at[d, p], dn_r.at[d, p], below)

    def up_arrived(d, p):
        block = wbuf.at[wrap(y - d - 1), place(p)]
        copy(block, block, up_s.at[d, p], up_r.at[d, p], above).wait_recv()

    def down_arrived(d, p):
        block = wbuf.at[wrap(y + d + 1), place(p)]
        copy(block, block, dn_s.at[d, p], dn_r.at[d, p], below).wait_recv()

    def first(p, carry):
        @pl.when(p != 0)
        def _():
            block = wbuf.at[y, place(p)]
            copy(block, block, s1_s.at[p], s1_r.at[p], above).wait_recv()

        up_copy(0, p).start()
        down_copy(0, p).start()
        return carry

    lax.fori_loop(0, SIDE, first, 0)

    for d in (1, 2):

        def onward(p, carry, d=d):
            up_arrived(d - 1, p)
            up_copy(d, p).start()
            down_arrived(d - 1, p)
            down_copy(d, p).start()
            return carry

        lax.fori_loop(0, SIDE, onward, 0)

    half = SIDE // 2

    def last(p, carry):
        up_arrived(2, p)
        up_copy(3, p).start()
        down_arrived(2, p)
        up_arrived(2, p + half)
        down_arrived(2, p + half)
        down_copy(3, p + half).start()
        return carry

    lax.fori_loop(0, half, last, 0)

    for i in ORDER:
        here = pl.ds(i * PAIR, PAIR)
        copy(sendb.at[here], recv.at[here], d_s.at[i], d_r.at[i], target(i)).wait_recv()
    for i in range(0, BLOCKS, 2):
        both = recv[pl.ds(i * PAIR, 2 * PAIR)].astype(F32)
        here = pl.ds(i * CAP, 2 * CAP)
        xs[here] = jnp.concatenate(
            [both[0:CAP], both[PAIR : PAIR + CAP]], axis=0
        ).astype(BF16)
        gs[here] = jnp.concatenate(
            [both[CAP:PAIR], both[PAIR + CAP : 2 * PAIR]], axis=0
        ).astype(BF16)

    def final(p, carry):
        up_arrived(3, p)
        down_arrived(3, p + half)
        return carry

    lax.fori_loop(0, half, final, 0)

    def weight(which):
        return wbuf[:, :, which].reshape(WIDTH, FF)

    gate_w, up_w, down_w = weight(0), weight(1), weight(2)
    x_rows, g_rows = xs[...], gs[...]
    gate = mm(x_rows, gate_w)
    up = mm(x_rows, up_w)
    sig = jax.nn.sigmoid(gate)
    act = gate * sig
    hidden = (act * up).astype(BF16)
    dw = mm_tn(g_rows, hidden)
    dwb[...] = dw.astype(BF16).reshape(SIDE, SIDE * SHARD, FF)

    def sum_copy(o):
        to = wrap(y + o)
        return copy(dwb.at[to], rs1.at[o], q_s.at[o], q_r.at[o], {"y": to})

    for o in (4, 3, 5, 2, 6, 1, 7):
        sum_copy(o).start()
    hid_grad = mm(g_rows, down_w)
    gate_grad = (hid_grad * up * (sig * (1.0 + gate * (1.0 - sig)))).astype(BF16)
    up_grad = (hid_grad * act).astype(BF16)

    def result_copy(i):
        here = pl.ds(i * PAIR, PAIR)
        return copy(outb.at[here], back.at[here], b_s.at[i], b_r.at[i], origin(i))

    part_rows = 4 * CAP
    for part in (2, 1, 3, 0):
        rows = slice(part * part_rows, (part + 1) * part_rows)
        made = mm_nt(hidden[rows], down_w)
        grad = mm_nt(gate_grad[rows], gate_w) + mm_nt(up_grad[rows], up_w)
        pieces = []
        for j in range(4):
            pieces.append(made[j * CAP : (j + 1) * CAP])
            pieces.append(grad[j * CAP : (j + 1) * CAP])
        outb[pl.ds(part * 4 * PAIR, 4 * PAIR)] = jnp.concatenate(pieces, axis=0).astype(
            BF16
        )
        for i in ORDER:
            if i // 4 == part:
                result_copy(i).start()
    back[pl.ds(0, PAIR)] = outb[pl.ds(0, PAIR)]

    total = dwb[y].astype(F32)
    for o in (1, 7, 2, 6, 3, 5, 4):
        sum_copy(o).wait_recv()
        total = total + rs1[o].astype(F32)
    s1b[...] = total.astype(BF16).reshape(SIDE, SHARD, FF)

    def row_sum_copy(o):
        to = wrap(x + o)
        return copy(s1b.at[to], rs2.at[o], t_s.at[o], t_r.at[o], {"x": to})

    for o in (4, 3, 5, 2, 6, 1, 7):
        row_sum_copy(o).start()
    same, other = s1b[x].astype(F32), None
    for o in range(1, SIDE):
        row_sum_copy(o).wait_recv()
        term = rs2[o].astype(F32)
        if o % 2 == 0:
            same = same + term
        else:
            other = term if other is None else other + term
    pz[0] = same
    pz[1] = other
    trade = copy(pz.at[1 - mix], pzr, e_s, e_r, partner)
    trade.start()

    for i in ORDER:
        result_copy(i).wait_recv()
    rows_back = back[...]
    out0, out1 = mm(gx[0], rows_back), mm(gx[1], rows_back)
    out_ref[...] = (r0 * out0 + r1 * out1).astype(BF16)
    tg_ref[...] = mm(gx[2] + gx[3], rows_back).astype(BF16)

    trade.wait_recv()
    dg_ref[0] = (pz[mix] + pzr[...]) * (1.0 / (SIDE * SIDE))

    swap.wait_send()
    trade.wait_send()
    for which in (0, 1):
        for i in range(4):
            off, sent = row_copy(which, i)
            if i == 0:

                @pl.when(off != 0)
                def _():
                    sent.wait_send()
            else:
                sent.wait_send()
    for d in (0, 1, 2):

        def drained(p, carry, d=d):
            up_copy(d, p).wait_send()
            down_copy(d, p).wait_send()
            return carry

        lax.fori_loop(0, SIDE, drained, 0)

    def drained_last(p, carry):
        up_copy(3, p).wait_send()
        down_copy(3, p + half).wait_send()
        return carry

    lax.fori_loop(0, half, drained_last, 0)
    for i in ORDER:
        here = pl.ds(i * PAIR, PAIR)
        copy(sendb.at[here], recv.at[here], d_s.at[i], d_r.at[i], target(i)).wait_send()
        result_copy(i).wait_send()
    for o in range(1, SIDE):
        sum_copy(o).wait_send()
        row_sum_copy(o).wait_send()


def local(tokens, expert_ids, routing, w_gate, w_up, w_down, grad_out):
    n_tok = tokens.shape[0]
    vmem = pl.BlockSpec(memory_space=pltpu.VMEM)
    dma = pltpu.SemaphoreType.DMA
    return pl.pallas_call(
        kernel,
        out_shape=(
            jax.ShapeDtypeStruct((n_tok, WIDTH), BF16),
            jax.ShapeDtypeStruct((n_tok, WIDTH), BF16),
            jax.ShapeDtypeStruct((1, SHARD, FF), F32),
        ),
        in_specs=[vmem] * 7,
        out_specs=(vmem, vmem, vmem),
        scratch_shapes=[
            pltpu.VMEM((2, 3, SHARD, FF), BF16),
            pltpu.VMEM((SIDE, SIDE, 3, SHARD, FF), BF16),
            pltpu.VMEM((BLOCKS * PAIR, WIDTH), BF16),
            pltpu.VMEM((BLOCKS * PAIR, WIDTH), BF16),
            pltpu.VMEM((ROWS, WIDTH), BF16),
            pltpu.VMEM((ROWS, WIDTH), BF16),
            pltpu.VMEM((BLOCKS * PAIR, WIDTH), BF16),
            pltpu.VMEM((BLOCKS * PAIR, WIDTH), BF16),
            pltpu.VMEM((SIDE, SIDE * SHARD, FF), BF16),
            pltpu.VMEM((SIDE, SIDE * SHARD, FF), BF16),
            pltpu.VMEM((SIDE, SHARD, FF), BF16),
            pltpu.VMEM((SIDE, SHARD, FF), BF16),
            pltpu.VMEM((2, SHARD, FF), F32),
            pltpu.VMEM((SHARD, FF), F32),
            pltpu.VMEM((4, n_tok, BLOCKS * PAIR), BF16),
            dma,
            dma,
            dma((SIDE,)),
            dma((SIDE,)),
            dma((4, SIDE)),
            dma((4, SIDE)),
            dma((4, SIDE)),
            dma((4, SIDE)),
            dma((BLOCKS,)),
            dma((BLOCKS,)),
            dma((BLOCKS,)),
            dma((BLOCKS,)),
            dma((SIDE,)),
            dma((SIDE,)),
            dma((SIDE,)),
            dma((SIDE,)),
            dma,
            dma,
        ],
        compiler_params=pltpu.CompilerParams(
            collective_id=0,
            has_side_effects=True,
            vmem_limit_bytes=48 * 1024 * 1024,
        ),
        cost_estimate=pl.CostEstimate(
            flops=3_000_000_000, bytes_accessed=2_000_000, transcendentals=150_000
        ),
    )(tokens, expert_ids, routing, w_gate, w_up, w_down, grad_out)


def solution(mesh):
    finer = Mesh(mesh.devices.reshape(SIDE, SIDE, SIDE, 2), ("y", "x", "z", "c"))
    every = ("y", "x", "z", "c")
    rows = P(every, None)
    weights = P(("z", "c"), ("y", "x"), None)
    return jax.shard_map(
        local,
        mesh=finer,
        in_specs=(rows, rows, rows, weights, weights, weights, rows),
        out_specs=(rows, rows, weights),
        check_vma=False,
    )
```

time: 217 us -> 99.7 us (0.46)
  the two profiles are of different devices: /device:TPU:2 before, /device:TPU:1 now
where the time goes in v1:
time: 99.7 us; the launch traced here: 99.4 us
  Pallas kernels  93.3 us (94%)
  local copies, waits for them, and re-layouts  5.43 us (5%)
    pallas_call x1, Pallas kernels, local(): pl.pallas_call(kernel, out_shape=(jax.ShapeDtypeStruct((n_tok, WIDTH), BF...  93.3 us
    unnamed x17, local copies, waits for them, and re-layouts  5.43 us

profile of v1, /device:TPU:1, one launch (start us, length us, event | category | flops | bytes accessed | tf_op | source)
XLA Modules:
  0.0 99.4 jit_solution(13430522433405983303)
XLA Ops:
  0.6 0.0 copy-start.5
  0.6 0.8 copy.10.ids_ref
  1.4 0.0 copy-done.5
  1.4 0.0 copy-start.2
  1.4 0.0 copy-start.3
  1.5 0.0 copy-start.4
  1.5 0.1 copy.11.rout_ref
  1.6 0.6 copy-done.2
  2.1 0.0 copy-done.3
  2.2 0.0 copy-done.4
  2.2 0.0 copy-start
  2.2 0.9 copy-done
  3.1 0.0 copy-start.1
  3.1 0.9 copy-done.1
  4.1 93.3 %shard_map.94 = (bf16[128,1024]{1,0:T(8,128)(2,1)S(1)}, bf16[128,1024]{1,0:T(8,128)(2,1)S(1)}, f32[1,16,384]{2,1,0:T(8,128)S(1)}) custom-call(bf16[128,1024]{1,0:T(8,128)(2,1)S(1)} %copy-done, s32[128,2]{1,0:T(8,128)S(1)} %copy.10.ids_ref, f32[128,2]{1,0:T(8,128)S(1)} %copy.11.rout_ref, bf16[1,16,384]{2,1,0:T(8,128)(2,1)S(1)} %copy-done.2, ...), custom_call_target="tpu_custom_call" | custom-call | flops 3000000000 | bytes 2000000 | tf_op jit(solution)/shard_map/pallas_call | solution.py:408
  97.4 0.7 copy.15
  98.1 0.7 copy.16
  98.8 0.6 copy.17
Async XLA Ops:
  0.6 0.8 copy-start.5
  1.4 0.7 copy-start.2
  1.4 0.7 copy-start.3
  1.5 0.7 copy-start.4
  2.2 0.9 copy-start
  3.1 0.9 copy-start.1

commit v2 on v1

v2 whole, which is shorter than its diff:
```python
import jax
import jax.numpy as jnp
from jax import lax
from jax.experimental import pallas as pl
from jax.experimental.pallas import tpu as pltpu
from jax.sharding import Mesh
from jax.sharding import PartitionSpec as P

MESH = pl.DeviceIdType.MESH
F32 = jnp.float32
BF16 = jnp.bfloat16
SIDE = 8
BLOCKS = 16
CAP = 24
PAIR = 2 * CAP
ROWS = BLOCKS * CAP
WIDTH = 1024
FF = 384
SHARD = 16
WIDE = 256
ORDER = (8, 9, 10, 11, 4, 5, 6, 7, 12, 13, 14, 15, 2, 3, 1)


def mm(a, b):
    return jnp.dot(a, b, preferred_element_type=F32)


def mm_nt(a, b):
    return lax.dot_general(a, b, (((1,), (1,)), ((), ())), preferred_element_type=F32)


def mm_tn(a, b):
    return lax.dot_general(a, b, (((0,), (0,)), ((), ())), preferred_element_type=F32)


def kernel(
    tok_any,
    ids_any,
    rout_any,
    wg_any,
    wu_any,
    wd_any,
    go_any,
    out_ref,
    tg_ref,
    dg_ref,
    tok,
    cot_in,
    ids_v,
    rout_v,
    sh,
    wbuf,
    sendb,
    recv,
    xs,
    gs,
    gst,
    acc,
    outb,
    back,
    dwy,
    ry1,
    sy1,
    ry2,
    dwx,
    rx1,
    sx1,
    rx2,
    back_mark,
    in_s,
    p_s,
    p_r,
    s1_s,
    s1_r,
    up_s,
    up_r,
    dn_s,
    dn_r,
    d_s,
    d_r,
    b_s,
    b_r,
    y1_s,
    y1_r,
    y2_s,
    y2_r,
    x1_s,
    x1_r,
    x2_s,
    x2_r,
):
    y, x = lax.axis_index("y"), lax.axis_index("x")
    z, c = lax.axis_index("z"), lax.axis_index("c")

    def wrap(v):
        return lax.rem(v + 2 * SIDE, SIDE)

    far = wrap(z + 4)
    partner = {"z": far}
    mix = lax.rem(z // 4 + lax.rem(x, 2), 2)

    def steps(i, core):
        k, f = i // 4, (i // 2) % 2
        way = 1 - 2 * core
        dz = (0, 1, 2 * way, -1)[k]
        return dz, f * way, i % 2

    def target(i):
        dz, dx, m = steps(i, c)
        return {"x": wrap(x + dx), "z": wrap(z + dz), "c": lax.rem(c + m, 2)}

    def origin(i):
        m = i % 2
        core = lax.rem(c + m, 2)
        dz, dx, _ = steps(i, core)
        return {"x": wrap(x - dx), "z": wrap(z - dz), "c": core}

    def copy(src, dst, send, recv_sem, device):
        return pltpu.make_async_remote_copy(
            src_ref=src,
            dst_ref=dst,
            send_sem=send,
            recv_sem=recv_sem,
            device_id=device,
            device_id_type=MESH,
        )

    barrier = pltpu.get_barrier_semaphore()

    def greet(device):
        pl.semaphore_signal(barrier, inc=1, device_id=device, device_id_type=MESH)

    loads = []
    for n, (src, dst) in enumerate(
        (
            (wg_any.at[0], sh.at[0, 0]),
            (wu_any.at[0], sh.at[0, 1]),
            (wd_any.at[0], sh.at[0, 2]),
            (ids_any, ids_v),
            (rout_any, rout_v),
            (tok_any, tok),
            (go_any, cot_in),
        )
    ):
        load = pltpu.make_async_copy(src, dst, in_s.at[n])
        load.start()
        loads.append(load)

    greet(partner)
    for o in range(1, SIDE):
        greet({"x": wrap(x + o)})
        greet({"y": wrap(y + o)})
        greet({"x": wrap(x + o), "z": far})
        greet({"y": wrap(y + o), "z": far})
    for i in range(1, BLOCKS):
        greet(target(i))
        greet(origin(i))
    for load in loads[:3]:
        load.wait()
    pl.semaphore_wait(barrier, 2 * (BLOCKS - 1) + 4 * (SIDE - 1) + 1)

    swap = copy(sh.at[0], sh.at[1], p_s, p_r, partner)
    swap.start()

    def row_copy(which, i):
        off = 2 * i + (mix if which == 0 else 1 - mix)
        dest = {"x": lax.rem(x + off, SIDE)}
        return off, copy(
            sh.at[which], wbuf.at[y, x], s1_s.at[off], s1_r.at[off], dest
        )

    def row_sends(which):
        for i in range(4):
            off, sent = row_copy(which, i)
            if i == 0:

                @pl.when(off == 0)
                def _():
                    wbuf[y, x] = sh[which]

                @pl.when(off != 0)
                def _():
                    sent.start()
            else:
                sent.start()

    row_sends(0)

    above, below = {"y": wrap(y + 1)}, {"y": wrap(y - 1)}

    def away(j):
        odd = lax.rem(j, 2)
        return odd * ((j + 1) // 2) + (1 - odd) * lax.rem(SIDE - j // 2, SIDE)

    def place(j):
        return lax.rem(x - away(j) + SIDE, SIDE)

    def up_copy(d, j):
        block = wbuf.at[wrap(y - d), place(j)]
        return copy(block, block, up_s.at[d, j], up_r.at[d, j], above)

    def down_copy(d, j):
        block = wbuf.at[wrap(y + d), place(j)]
        return copy(block, block, dn_s.at[d, j], dn_r.at[d, j], below)

    def up_arrived(d, j):
        block = wbuf.at[wrap(y - d - 1), place(j)]
        copy(block, block, up_s.at[d, j], up_r.at[d, j], above).wait_recv()

    def down_arrived(d, j):
        block = wbuf.at[wrap(y + d + 1), place(j)]
        copy(block, block, dn_s.at[d, j], dn_r.at[d, j], below).wait_recv()

    @pl.when(mix == 0)
    def _():
        up_copy(0, 0).start()
        down_copy(0, 0).start()

    for load in loads[3:]:
        load.wait()
    id0, id1 = ids_v[0:1], ids_v[1:2]
    n_tok = id0.shape[1]
    names = lax.broadcasted_iota(jnp.int32, (16, n_tok), 0)
    named = jnp.where((names == id0) | (names == id1), 1.0, 0.0).astype(BF16)
    row_i = lax.broadcasted_iota(jnp.int32, (n_tok, n_tok), 0)
    col_i = lax.broadcasted_iota(jnp.int32, (n_tok, n_tok), 1)
    before = mm(named, jnp.where(row_i < col_i, 1.0, 0.0).astype(BF16))

    def slot_of(expert):
        rank = jnp.sum(jnp.where(names == expert, before, 0.0), axis=0, keepdims=True)
        k = ((expert >> 1) - z + SIDE) & 3
        f = ((expert >> 3) + x) & 1
        m = (expert + c) & 1
        return (k * 4 + f * 2 + m) * PAIR + rank.astype(jnp.int32)

    slot0, slot1 = slot_of(id0), slot_of(id1)

    def mark(first, count, slot):
        slots = lax.broadcasted_iota(jnp.int32, (count, n_tok), 0) + first
        return jnp.where(slots == slot, 1.0, 0.0)

    def column(row):
        return jnp.transpose(jnp.broadcast_to(row, (n_tok, n_tok)))[:, 0:1]

    r0, r1 = column(rout_v[0:1]), column(rout_v[1:2])
    cot = cot_in[...].astype(F32)
    staged = jnp.concatenate(
        [tok[...], (r0 * cot).astype(BF16), (r1 * cot).astype(BF16)], axis=0
    )

    quarter = BLOCKS * PAIR // 4

    def pack(part):
        first = part * quarter
        m0, m1 = mark(first, quarter, slot0), mark(first, quarter, slot1)
        g0 = mark(first, quarter, slot0 + CAP)
        g1 = mark(first, quarter, slot1 + CAP)
        chosen = jnp.concatenate(
            [(m0 + m1).astype(BF16), g0.astype(BF16), g1.astype(BF16)], axis=1
        )
        sendb[pl.ds(first, quarter)] = mm(chosen, staged).astype(BF16)
        for i in ORDER:
            if i // 4 == part:
                here = pl.ds(i * PAIR, PAIR)
                copy(
                    sendb.at[here], recv.at[here], d_s.at[i], d_r.at[i], target(i)
                ).start()

    pack(2)
    swap.wait_recv()
    row_sends(1)

    @pl.when(mix == 1)
    def _():
        up_copy(0, 0).start()
        down_copy(0, 0).start()

    pack(1)
    pack(3)
    pack(0)
    recv[pl.ds(0, PAIR)] = sendb[pl.ds(0, PAIR)]

    def first_step(j, carry):
        block = wbuf.at[y, place(j)]
        copy(block, block, s1_s.at[away(j)], s1_r.at[away(j)], above).wait_recv()
        up_copy(0, j).start()
        down_copy(0, j).start()
        return carry

    lax.fori_loop(1, SIDE, first_step, 0)

    for d in (1, 2):

        def onward(p, carry, d=d):
            up_arrived(d - 1, p)
            up_copy(d, p).start()
            down_arrived(d - 1, p)
            down_copy(d, p).start()
            return carry

        lax.fori_loop(0, SIDE, onward, 0)

    half = SIDE // 2

    def last(p, carry):
        up_arrived(2, p)
        up_copy(3, p).start()
        down_arrived(2, p)
        up_arrived(2, p + half)
        down_arrived(2, p + half)
        down_copy(3, p + half).start()
        return carry

    lax.fori_loop(0, half, last, 0)

    for i in ORDER:
        here = pl.ds(i * PAIR, PAIR)
        copy(sendb.at[here], recv.at[here], d_s.at[i], d_r.at[i], target(i)).wait_recv()
    for i in range(0, BLOCKS, 2):
        both = recv[pl.ds(i * PAIR, 2 * PAIR)].astype(F32)
        here = pl.ds(i * CAP, 2 * CAP)
        xs[here] = jnp.concatenate(
            [both[0:CAP], both[PAIR : PAIR + CAP]], axis=0
        ).astype(BF16)
        gs[here] = jnp.concatenate(
            [both[CAP:PAIR], both[PAIR + CAP : 2 * PAIR]], axis=0
        ).astype(BF16)

    depth = SIDE * SHARD

    def accumulate(shifts, start):
        blocks = [wrap(y + s) for s in shifts]
        cols = [pl.ds(pl.multiple_of(b * depth, depth), depth) for b in blocks]
        x_part = jnp.concatenate([xs[:, at] for at in cols], axis=1)
        g_part = jnp.concatenate([gs[:, at] for at in cols], axis=1)
        for which, rows in ((0, x_part), (1, x_part), (2, g_part)):
            held = jnp.concatenate(
                [wbuf[b, :, which].reshape(depth, FF) for b in blocks], axis=0
            )
            term = mm(rows, held)
            acc[which] = term if start else acc[which] + term

    accumulate((0, 1), True)
    accumulate((-1, 2), False)
    accumulate((-2, 3), False)
    accumulate((-3,), False)
    gst[...] = jnp.transpose(gs[...])
    for k in range(3):
        whole = (
            mark(0, BLOCKS * PAIR, slot0)
            if k == 0
            else mark(0, BLOCKS * PAIR, slot1)
            if k == 1
            else mark(0, BLOCKS * PAIR, slot0 + CAP)
            + mark(0, BLOCKS * PAIR, slot1 + CAP)
        )
        back_mark[pl.ds(k * n_tok, n_tok)] = jnp.transpose(whole).astype(BF16)

    def final(p, carry):
        up_arrived(3, p)
        down_arrived(3, p + half)
        return carry

    lax.fori_loop(0, half, final, 0)
    accumulate((4,), False)

    def weight(which):
        return wbuf[:, :, which].reshape(WIDTH, FF)

    gate_w, up_w, down_w = weight(0), weight(1), weight(2)
    gate, up = acc[0], acc[1]
    sig = jax.nn.sigmoid(gate)
    act = gate * sig
    hidden = (act * up).astype(BF16)

    dw = mm(gst[...], hidden).astype(BF16)
    dwy[...] = dw[:, 0:WIDE].reshape(SIDE, SIDE * SHARD, WIDE)
    dwx[...] = dw[:, WIDE:FF].reshape(SIDE, SIDE, SHARD, FF - WIDE)

    def y1_copy(o):
        to = wrap(y + o)
        return copy(dwy.at[to], ry1.at[o], y1_s.at[o], y1_r.at[o], {"y": to})

    def x1_copy(o):
        to = wrap(x + o)
        return copy(dwx.at[:, to], rx1.at[o], x1_s.at[o], x1_r.at[o], {"x": to})

    for o in (4, 3, 5, 2, 6, 1, 7):
        y1_copy(o).start()
        x1_copy(o).start()
    hid_grad = acc[2]
    gate_grad = (hid_grad * up * (sig * (1.0 + gate * (1.0 - sig)))).astype(BF16)
    up_grad = (hid_grad * act).astype(BF16)

    def result_copy(i):
        here = pl.ds(i * PAIR, PAIR)
        return copy(outb.at[here], back.at[here], b_s.at[i], b_r.at[i], origin(i))

    part_rows = 4 * CAP
    for part in (2, 1, 3, 0):
        rows = slice(part * part_rows, (part + 1) * part_rows)
        made = mm_nt(hidden[rows], down_w)
        grad = mm_nt(gate_grad[rows], gate_w) + mm_nt(up_grad[rows], up_w)
        pieces = []
        for j in range(4):
            pieces.append(made[j * CAP : (j + 1) * CAP])
            pieces.append(grad[j * CAP : (j + 1) * CAP])
        outb[pl.ds(part * 4 * PAIR, 4 * PAIR)] = jnp.concatenate(pieces, axis=0).astype(
            BF16
        )
        for i in ORDER:
            if i // 4 == part:
                result_copy(i).start()
    back[pl.ds(0, PAIR)] = outb[pl.ds(0, PAIR)]

    total = dwy[y].astype(F32)
    for o in (1, 7, 2, 6, 3, 5, 4):
        y1_copy(o).wait_recv()
        total = total + ry1[o].astype(F32)
    sy1[...] = total.astype(BF16).reshape(SIDE, SHARD, WIDE)

    own_plane = wrap(z + 4 * mix)

    def y2_copy(o):
        to = wrap(x + o)
        slot = 2 * (o // 2) + mix
        return copy(
            sy1.at[to],
            ry2.at[slot],
            y2_s.at[o],
            y2_r.at[slot],
            {"x": to, "z": own_plane},
        )

    y2_copy_self = y2_copy(0)

    @pl.when(mix == 0)
    def _():
        ry2[0] = sy1[x]

    @pl.when(mix == 1)
    def _():
        y2_copy_self.start()

    for o in (4, 3, 5, 2, 6, 1, 7):
        y2_copy(o).start()

    same = dwx[:, x].astype(F32)
    other = None
    for o in (1, 7, 2, 6, 3, 5, 4):
        x1_copy(o).wait_recv()
        term = rx1[o].astype(F32)
        if o % 2 == 0:
            same = same + term
        else:
            other = term if other is None else other + term
    sx1[0] = same.astype(BF16)
    sx1[1] = other.astype(BF16)

    def x2_copy(which, o):
        to = wrap(y + o)
        held = lax.rem(mix + which, 2)
        return copy(
            sx1.at[held, to],
            rx2.at[which, o],
            x2_s.at[which, o],
            x2_r.at[which, o],
            {"y": to, "z": wrap(z + 4 * which)},
        )

    rx2[0, 0] = sx1[mix, y]
    x2_copy(1, 0).start()
    for o in (4, 3, 5, 2, 6, 1, 7):
        x2_copy(0, o).start()
        x2_copy(1, o).start()

    for i in ORDER:
        result_copy(i).wait_recv()
    from_mark = mm(back_mark[...], back[...])
    out_ref[...] = (r0 * from_mark[0:n_tok] + r1 * from_mark[n_tok : 2 * n_tok]).astype(
        BF16
    )
    tg_ref[...] = from_mark[2 * n_tok : 3 * n_tok].astype(BF16)

    def y2_arrived(slot):
        copy(
            sy1.at[0], ry2.at[slot], y2_s.at[0], y2_r.at[slot], {"z": own_plane}
        ).wait_recv()

    @pl.when(mix == 1)
    def _():
        y2_arrived(0)

    for slot in range(1, SIDE):
        y2_arrived(slot)
    for o in range(SIDE):
        for which in (0, 1):
            if o or which:
                x2_copy(which, o).wait_recv()
    scale = 1.0 / (SIDE * SIDE)
    wide = ry2[0].astype(F32)
    for slot in range(1, SIDE):
        wide = wide + ry2[slot].astype(F32)
    narrow = None
    for o in range(SIDE):
        for which in (0, 1):
            term = rx2[which, o].astype(F32)
            narrow = term if narrow is None else narrow + term
    dg_ref[0] = jnp.concatenate([wide, narrow], axis=1) * scale

    swap.wait_send()
    for which in (0, 1):
        for i in range(4):
            off, sent = row_copy(which, i)
            if i == 0:

                @pl.when(off != 0)
                def _():
                    sent.wait_send()
            else:
                sent.wait_send()
    for d in (0, 1, 2):

        def drained(p, carry, d=d):
            up_copy(d, p).wait_send()
            down_copy(d, p).wait_send()
            return carry

        lax.fori_loop(0, SIDE, drained, 0)

    def drained_last(p, carry):
        up_copy(3, p).wait_send()
        down_copy(3, p + half).wait_send()
        return carry

    lax.fori_loop(0, half, drained_last, 0)
    for i in ORDER:
        here = pl.ds(i * PAIR, PAIR)
        copy(sendb.at[here], recv.at[here], d_s.at[i], d_r.at[i], target(i)).wait_send()
        result_copy(i).wait_send()

    @pl.when(mix == 1)
    def _():
        y2_copy_self.wait_send()

    x2_copy(1, 0).wait_send()
    for o in range(1, SIDE):
        y1_copy(o).wait_send()
        x1_copy(o).wait_send()
        y2_copy(o).wait_send()
        x2_copy(0, o).wait_send()
        x2_copy(1, o).wait_send()


def local(tokens, expert_ids, routing, w_gate, w_up, w_down, grad_out):
    n_tok = tokens.shape[0]
    vmem = pl.BlockSpec(memory_space=pltpu.VMEM)
    hbm = pl.BlockSpec(memory_space=pltpu.HBM)
    dma = pltpu.SemaphoreType.DMA
    narrow = FF - WIDE
    return pl.pallas_call(
        kernel,
        out_shape=(
            jax.ShapeDtypeStruct((n_tok, WIDTH), BF16),
            jax.ShapeDtypeStruct((n_tok, WIDTH), BF16),
            jax.ShapeDtypeStruct((1, SHARD, FF), F32),
        ),
        in_specs=[hbm] * 7,
        out_specs=(vmem, vmem, vmem),
        scratch_shapes=[
            pltpu.VMEM((n_tok, WIDTH), BF16),
            pltpu.VMEM((n_tok, WIDTH), BF16),
            pltpu.VMEM((2, n_tok), jnp.int32),
            pltpu.VMEM((2, n_tok), F32),
            pltpu.VMEM((2, 3, SHARD, FF), BF16),
            pltpu.VMEM((SIDE, SIDE, 3, SHARD, FF), BF16),
            pltpu.VMEM((BLOCKS * PAIR, WIDTH), BF16),
            pltpu.VMEM((BLOCKS * PAIR, WIDTH), BF16),
            pltpu.VMEM((ROWS, WIDTH), BF16),
            pltpu.VMEM((ROWS, WIDTH), BF16),
            pltpu.VMEM((WIDTH, ROWS), BF16),
            pltpu.VMEM((3, ROWS, FF), F32),
            pltpu.VMEM((BLOCKS * PAIR, WIDTH), BF16),
            pltpu.VMEM((BLOCKS * PAIR, WIDTH), BF16),
            pltpu.VMEM((SIDE, SIDE * SHARD, WIDE), BF16),
            pltpu.VMEM((SIDE, SIDE * SHARD, WIDE), BF16),
            pltpu.VMEM((SIDE, SHARD, WIDE), BF16),
            pltpu.VMEM((SIDE, SHARD, WIDE), BF16),
            pltpu.VMEM((SIDE, SIDE, SHARD, narrow), BF16),
            pltpu.VMEM((SIDE, SIDE, SHARD, narrow), BF16),
            pltpu.VMEM((2, SIDE, SHARD, narrow), BF16),
            pltpu.VMEM((2, SIDE, SHARD, narrow), BF16),
            pltpu.VMEM((3 * n_tok, BLOCKS * PAIR), BF16),
            dma((7,)),
            dma,
            dma,
            dma((SIDE,)),
            dma((SIDE,)),
            dma((4, SIDE)),
            dma((4, SIDE)),
            dma((4, SIDE)),
            dma((4, SIDE)),
            dma((BLOCKS,)),
            dma((BLOCKS,)),
            dma((BLOCKS,)),
            dma((BLOCKS,)),
            dma((SIDE,)),
            dma((SIDE,)),
            dma((SIDE,)),
            dma((SIDE,)),
            dma((SIDE,)),
            dma((SIDE,)),
            dma((2, SIDE)),
            dma((2, SIDE)),
        ],
        compiler_params=pltpu.CompilerParams(
            collective_id=0,
            has_side_effects=True,
            vmem_limit_bytes=56 * 1024 * 1024,
        ),
        cost_estimate=pl.CostEstimate(
            flops=3_000_000_000, bytes_accessed=2_000_000, transcendentals=150_000
        ),
    )(tokens, expert_ids.T, routing.T, w_gate, w_up, w_down, grad_out)


def solution(mesh):
    finer = Mesh(mesh.devices.reshape(SIDE, SIDE, SIDE, 2), ("y", "x", "z", "c"))
    every = ("y", "x", "z", "c")
    rows = P(every, None)
    weights = P(("z", "c"), ("y", "x"), None)
    return jax.shard_map(
        local,
        mesh=finer,
        in_specs=(rows, rows, rows, weights, weights, weights, rows),
        out_specs=(rows, rows, weights),
        check_vma=False,
    )
```

time: 99.7 us -> 89.6 us (0.90)
  Pallas kernels: 93.3 us -> 85.6 us
  local copies, waits for them, and re-layouts: 5.43 us -> 3.06 us
    pallas_call x1, Pallas kernels: 93.3 us -> 85.6 us  [local(): pl.pallas_call(kernel, out_shape=(jax.ShapeDtypeStruct((n_tok, WIDTH), BF...]
    unnamed x17 -> x7, local copies, waits for them, and re-layouts: 5.43 us -> 3.06 us
where the time goes in v2:
time: 89.6 us; the launch traced here: 89.3 us
  Pallas kernels  85.6 us (96%)
  local copies, waits for them, and re-layouts  3.06 us (3%)
    pallas_call x1, Pallas kernels, local(): pl.pallas_call(kernel, out_shape=(jax.ShapeDtypeStruct((n_tok, WIDTH), BF...  85.6 us
    unnamed x7, local copies, waits for them, and re-layouts  3.06 us

profile of v2, /device:TPU:1, one launch (start us, length us, event | category | flops | bytes accessed | tf_op | source)
XLA Modules:
  0.0 89.3 jit_solution(9852734595773938347)
XLA Ops:
  0.6 85.6 %shard_map.94 = (bf16[128,1024]{1,0:T(8,128)(2,1)}, bf16[128,1024]{1,0:T(8,128)(2,1)}, f32[1,16,384]{2,1,0:T(8,128)}) custom-call(bf16[128,1024]{1,0:T(8,128)(2,1)} %tok_any.1, s32[2,128]{1,0:T(2,128)} %bitcast.2, f32[2,128]{1,0:T(2,128)} %bitcast.3, bf16[1,16,384]{2,1,0:T(8,128)(2,1)} %wg_any.1, bf16[1,16,384]{2,1,0:T(8,128)(2,1)} %wu_any.1, ...), custom_call_target="tpu_custom_call" | custom-call | flops 3000000000 | bytes 2000000 | tf_op jit(solution)/shard_map/pallas_call | solution.py:561
  86.2 0.0 copy-start
  86.3 1.7 %copy.13 = bf16[128,1024]{1,0:T(8,128)(2,1)} copy(bf16[128,1024]{1,0:T(8,128)(2,1)} %get-tuple-element.6) | data formatting | bytes 524288
  88.0 0.0 copy-done
  88.0 0.0 copy-start.1
  88.0 0.7 copy.14
  88.7 0.0 copy-done.1
  88.7 0.6 copy.15
Async XLA Ops:
  86.2 1.7 %copy-start = (bf16[128,1024]{1,0:T(8,128)(2,1)S(1)}, bf16[128,1024]{1,0:T(8,128)(2,1)}, u32[]{:S(2)}) copy-start(bf16[128,1024]{1,0:T(8,128)(2,1)} %get-tuple-element.7) | copy-start | bytes 786436
  88.0 0.7 copy-start.1

commit v3 on v2

--- a/solution.py
+++ b/solution.py
@@ -195,26 +195,46 @@
     def place(j):
         return lax.rem(x - away(j) + SIDE, SIDE)
 
-    def up_copy(d, j):
-        block = wbuf.at[wrap(y - d), place(j)]
-        return copy(block, block, up_s.at[d, j], up_r.at[d, j], above)
-
-    def down_copy(d, j):
-        block = wbuf.at[wrap(y + d), place(j)]
-        return copy(block, block, dn_s.at[d, j], dn_r.at[d, j], below)
-
-    def up_arrived(d, j):
-        block = wbuf.at[wrap(y - d - 1), place(j)]
-        copy(block, block, up_s.at[d, j], up_r.at[d, j], above).wait_recv()
-
-    def down_arrived(d, j):
-        block = wbuf.at[wrap(y + d + 1), place(j)]
-        copy(block, block, dn_s.at[d, j], dn_r.at[d, j], below).wait_recv()
+    def ring_block(row, j, part):
+        return wbuf.at[wrap(row), place(j), pl.ds(2 * part, 2 - part)]
+
+    def up_copy(part, d, j):
+        block = ring_block(y - d, j, part)
+        return copy(block, block, up_s.at[part, d, j], up_r.at[part, d, j], above)
+
+    def down_copy(part, d, j):
+        block = ring_block(y + d, j, part)
+        return copy(block, block, dn_s.at[part, d, j], dn_r.at[part, d, j], below)
+
+    def up_arrived(part, d, j):
+        block = ring_block(y - d - 1, j, part)
+        copy(
+            block, block, up_s.at[part, d, j], up_r.at[part, d, j], above
+        ).wait_recv()
+
+    def down_arrived(part, d, j):
+        block = ring_block(y + d + 1, j, part)
+        copy(
+            block, block, dn_s.at[part, d, j], dn_r.at[part, d, j], below
+        ).wait_recv()
+
+    def first_step(j, carry):
+        block = wbuf.at[y, place(j)]
+        copy(block, block, s1_s.at[away(j)], s1_r.at[away(j)], above).wait_recv()
+        up_copy(0, 0, j).start()
+        down_copy(0, 0, j).start()
+        return carry
+
+    def first_steps(low, high):
+        lax.fori_loop(low, high, first_step, 0)
+
+    def first_own():
+        up_copy(0, 0, 0).start()
+        down_copy(0, 0, 0).start()
 
     @pl.when(mix == 0)
     def _():
-        up_copy(0, 0).start()
-        down_copy(0, 0).start()
+        first_own()
 
     for load in loads[3:]:
         load.wait()
@@ -266,52 +286,88 @@
                     sendb.at[here], recv.at[here], d_s.at[i], d_r.at[i], target(i)
                 ).start()
 
+    @pl.when(mix == 0)
+    def _():
+        first_steps(1, 3)
+
     pack(2)
     swap.wait_recv()
     row_sends(1)
 
     @pl.when(mix == 1)
     def _():
-        up_copy(0, 0).start()
-        down_copy(0, 0).start()
+        first_own()
+
+    @pl.when(mix == 0)
+    def _():
+        first_steps(3, 5)
 
     pack(1)
+
+    @pl.when(mix == 0)
+    def _():
+        first_steps(5, 7)
+
     pack(3)
+
+    @pl.when(mix == 1)
+    def _():
+        first_steps(1, 3)
+
     pack(0)
     recv[pl.ds(0, PAIR)] = sendb[pl.ds(0, PAIR)]
 
-    def first_step(j, carry):
-        block = wbuf.at[y, place(j)]
-        copy(block, block, s1_s.at[away(j)], s1_r.at[away(j)], above).wait_recv()
-        up_copy(0, j).start()
-        down_copy(0, j).start()
+    @pl.when(mix == 0)
+    def _():
+        first_steps(7, SIDE)
+
+    @pl.when(mix == 1)
+    def _():
+        first_steps(3, SIDE)
+
+    half = SIDE // 2
+
+    def onward(part, d):
+        def step(j, carry):
+            up_arrived(part, d - 1, j)
+            up_copy(part, d, j).start()
+            down_arrived(part, d - 1, j)
+            down_copy(part, d, j).start()
+            return carry
+
+        lax.fori_loop(0, SIDE, step, 0)
+
+    def onward_last(part):
+        def step(j, carry):
+            up_arrived(part, 2, j)
+            up_copy(part, 3, j).start()
+            down_arrived(part, 2, j)
+            up_arrived(part, 2, j + half)
+            down_arrived(part, 2, j + half)
+            down_copy(part, 3, j + half).start()
+            return carry
+
+        lax.fori_loop(0, half, step, 0)
+
+    def landed(part):
+        def step(j, carry):
+            up_arrived(part, 3, j)
+            down_arrived(part, 3, j + half)
+            return carry
+
+        lax.fori_loop(0, half, step, 0)
+
+    def down_first(j, carry):
+        up_copy(1, 0, j).start()
+        down_copy(1, 0, j).start()
         return carry
 
-    lax.fori_loop(1, SIDE, first_step, 0)
-
-    for d in (1, 2):
-
-        def onward(p, carry, d=d):
-            up_arrived(d - 1, p)
-            up_copy(d, p).start()
-            down_arrived(d - 1, p)
-            down_copy(d, p).start()
-            return carry
-
-        lax.fori_loop(0, SIDE, onward, 0)
-
-    half = SIDE // 2
-
-    def last(p, carry):
-        up_arrived(2, p)
-        up_copy(3, p).start()
-        down_arrived(2, p)
-        up_arrived(2, p + half)
-        down_arrived(2, p + half)
-        down_copy(3, p + half).start()
-        return carry
-
-    lax.fori_loop(0, half, last, 0)
+    onward(0, 1)
+    lax.fori_loop(0, SIDE, down_first, 0)
+    onward(0, 2)
+    onward(1, 1)
+    onward_last(0)
+    onward(1, 2)
 
     for i in ORDER:
         here = pl.ds(i * PAIR, PAIR)
@@ -328,23 +384,55 @@
 
     depth = SIDE * SHARD
 
-    def accumulate(shifts, start):
+    def accumulate(part, shifts, start):
         blocks = [wrap(y + s) for s in shifts]
         cols = [pl.ds(pl.multiple_of(b * depth, depth), depth) for b in blocks]
-        x_part = jnp.concatenate([xs[:, at] for at in cols], axis=1)
-        g_part = jnp.concatenate([gs[:, at] for at in cols], axis=1)
-        for which, rows in ((0, x_part), (1, x_part), (2, g_part)):
+        rows = gs if part else xs
+        rows = jnp.concatenate([rows[:, at] for at in cols], axis=1)
+        for which in (2,) if part else (0, 1):
             held = jnp.concatenate(
                 [wbuf[b, :, which].reshape(depth, FF) for b in blocks], axis=0
             )
             term = mm(rows, held)
             acc[which] = term if start else acc[which] + term
 
-    accumulate((0, 1), True)
-    accumulate((-1, 2), False)
-    accumulate((-2, 3), False)
-    accumulate((-3,), False)
+    def accumulate_near(part):
+        accumulate(part, (0, 1), True)
+        accumulate(part, (-1, 2), False)
+        accumulate(part, (-2, 3), False)
+        accumulate(part, (-3,), False)
+
+    accumulate_near(0)
+    onward_last(1)
     gst[...] = jnp.transpose(gs[...])
+    landed(0)
+    accumulate(0, (4,), False)
+
+    def weight(which):
+        return wbuf[:, :, which].reshape(WIDTH, FF)
+
+    gate, up = acc[0], acc[1]
+    sig = jax.nn.sigmoid(gate)
+    act = gate * sig
+    hidden = (act * up).astype(BF16)
+
+    dw = mm(gst[...], hidden).astype(BF16)
+    dwy[...] = dw[:, 0:WIDE].reshape(SIDE, SIDE * SHARD, WIDE)
+    dwx[...] = dw[:, WIDE:FF].reshape(SIDE, SIDE, SHARD, FF - WIDE)
+
+    def y1_copy(o):
+        to = wrap(y + o)
+        return copy(dwy.at[to], ry1.at[o], y1_s.at[o], y1_r.at[o], {"y": to})
+
+    def x1_copy(o):
+        to = wrap(x + o)
+        return copy(dwx.at[:, to], rx1.at[o], x1_s.at[o], x1_r.at[o], {"x": to})
+
+    for o in (4, 3, 5, 2, 6, 1, 7):
+        y1_copy(o).start()
+        x1_copy(o).start()
+
+    accumulate_near(1)
     for k in range(3):
         whole = (
             mark(0, BLOCKS * PAIR, slot0)
@@ -355,39 +443,9 @@
             + mark(0, BLOCKS * PAIR, slot1 + CAP)
         )
         back_mark[pl.ds(k * n_tok, n_tok)] = jnp.transpose(whole).astype(BF16)
-
-    def final(p, carry):
-        up_arrived(3, p)
-        down_arrived(3, p + half)
-        return carry
-
-    lax.fori_loop(0, half, final, 0)
-    accumulate((4,), False)
-
-    def weight(which):
-        return wbuf[:, :, which].reshape(WIDTH, FF)
-
+    landed(1)
+    accumulate(1, (4,), False)
     gate_w, up_w, down_w = weight(0), weight(1), weight(2)
-    gate, up = acc[0], acc[1]
-    sig = jax.nn.sigmoid(gate)
-    act = gate * sig
-    hidden = (act * up).astype(BF16)
-
-    dw = mm(gst[...], hidden).astype(BF16)
-    dwy[...] = dw[:, 0:WIDE].reshape(SIDE, SIDE * SHARD, WIDE)
-    dwx[...] = dw[:, WIDE:FF].reshape(SIDE, SIDE, SHARD, FF - WIDE)
-
-    def y1_copy(o):
-        to = wrap(y + o)
-        return copy(dwy.at[to], ry1.at[o], y1_s.at[o], y1_r.at[o], {"y": to})
-
-    def x1_copy(o):
-        to = wrap(x + o)
-        return copy(dwx.at[:, to], rx1.at[o], x1_s.at[o], x1_r.at[o], {"x": to})
-
-    for o in (4, 3, 5, 2, 6, 1, 7):
-        y1_copy(o).start()
-        x1_copy(o).start()
     hid_grad = acc[2]
     gate_grad = (hid_grad * up * (sig * (1.0 + gate * (1.0 - sig)))).astype(BF16)
     up_grad = (hid_grad * act).astype(BF16)
@@ -519,21 +577,22 @@
                     sent.wait_send()
             else:
                 sent.wait_send()
-    for d in (0, 1, 2):
-
-        def drained(p, carry, d=d):
-            up_copy(d, p).wait_send()
-            down_copy(d, p).wait_send()
+    for part in (0, 1):
+        for d in (0, 1, 2):
+
+            def drained(j, carry, part=part, d=d):
+                up_copy(part, d, j).wait_send()
+                down_copy(part, d, j).wait_send()
+                return carry
+
+            lax.fori_loop(0, SIDE, drained, 0)
+
+        def drained_last(j, carry, part=part):
+            up_copy(part, 3, j).wait_send()
+            down_copy(part, 3, j + half).wait_send()
             return carry
 
-        lax.fori_loop(0, SIDE, drained, 0)
-
-    def drained_last(p, carry):
-        up_copy(3, p).wait_send()
-        down_copy(3, p + half).wait_send()
-        return carry
-
-    lax.fori_loop(0, half, drained_last, 0)
+        lax.fori_loop(0, half, drained_last, 0)
     for i in ORDER:
         here = pl.ds(i * PAIR, PAIR)
         copy(sendb.at[here], recv.at[here], d_s.at[i], d_r.at[i], target(i)).wait_send()
@@ -552,13 +611,26 @@
         x2_copy(1, o).wait_send()
 
 
+def store(out_v, tg_v, dg_v, out_ref, tg_ref, dg_ref, sem):
+    moves = [
+        pltpu.make_async_copy(src, dst, sem.at[n])
+        for n, (src, dst) in enumerate(
+            ((out_v, out_ref), (tg_v, tg_ref), (dg_v, dg_ref))
+        )
+    ]
+    for move in moves:
+        move.start()
+    for move in moves:
+        move.wait()
+
+
 def local(tokens, expert_ids, routing, w_gate, w_up, w_down, grad_out):
     n_tok = tokens.shape[0]
     vmem = pl.BlockSpec(memory_space=pltpu.VMEM)
     hbm = pl.BlockSpec(memory_space=pltpu.HBM)
     dma = pltpu.SemaphoreType.DMA
     narrow = FF - WIDE
-    return pl.pallas_call(
+    made = pl.pallas_call(
         kernel,
         out_shape=(
             jax.ShapeDtypeStruct((n_tok, WIDTH), BF16),
@@ -596,10 +668,10 @@
             dma,
             dma((SIDE,)),
             dma((SIDE,)),
-            dma((4, SIDE)),
-            dma((4, SIDE)),
-            dma((4, SIDE)),
-            dma((4, SIDE)),
+            dma((2, 4, SIDE)),
+            dma((2, 4, SIDE)),
+            dma((2, 4, SIDE)),
+            dma((2, 4, SIDE)),
             dma((BLOCKS,)),
             dma((BLOCKS,)),
             dma((BLOCKS,)),
@@ -616,12 +688,33 @@
         compiler_params=pltpu.CompilerParams(
             collective_id=0,
             has_side_effects=True,
-            vmem_limit_bytes=56 * 1024 * 1024,
+            vmem_limit_bytes=44 * 1024 * 1024,
         ),
         cost_estimate=pl.CostEstimate(
             flops=3_000_000_000, bytes_accessed=2_000_000, transcendentals=150_000
         ),
-    )(tokens, expert_ids.T, routing.T, w_gate, w_up, w_down, grad_out)
+    )(
+        *(
+            pltpu.with_memory_space_constraint(a, pltpu.HBM)
+            for a in (
+                tokens,
+                expert_ids.T,
+                routing.T,
+                w_gate,
+                w_up,
+                w_down,
+                grad_out,
+            )
+        )
+    )
+    return pl.pallas_call(
+        store,
+        out_shape=[jax.ShapeDtypeStruct(a.shape, a.dtype) for a in made],
+        in_specs=[vmem] * 3,
+        out_specs=[hbm] * 3,
+        scratch_shapes=[dma((3,))],
+        compiler_params=pltpu.CompilerParams(vmem_limit_bytes=1024 * 1024),
+    )(*made)
 
 
 def solution(mesh):

time: 89.6 us -> 85.9 us (0.959)
  local copies, waits for them, and re-layouts: 3.06 us -> 0 us
    unnamed x7 -> x0, local copies, waits for them, and re-layouts: 3.06 us -> none
    pallas_call x1, Pallas kernels: 85.6 us -> 84.3 us  [local(): pl.pallas_call(kernel, out_shape=(jax.ShapeDtypeStruct((n_tok, WIDTH), BF...]
where the time goes in v3:
time: 85.9 us; the launch traced here: 85.7 us
  Pallas kernels  85.1 us (99%)
    pallas_call x1, Pallas kernels, local(): pl.pallas_call(kernel, out_shape=(jax.ShapeDtypeStruct((n_tok, WIDTH), BF...  84.3 us

profile of v3, /device:TPU:1, one launch (start us, length us, event | category | flops | bytes accessed | tf_op | source)
XLA Modules:
  0.0 85.7 jit_solution(13403999012130025135)
XLA Ops:
  0.6 84.3 %shard_map.94 = (bf16[128,1024]{1,0:T(8,128)(2,1)S(1)}, bf16[128,1024]{1,0:T(8,128)(2,1)S(1)}, f32[1,16,384]{2,1,0:T(8,128)S(1)}) custom-call(bf16[128,1024]{1,0:T(8,128)(2,1)} %tok_any.1, s32[2,128]{1,0:T(2,128)} %bitcast.2, f32[2,128]{1,0:T(2,128)} %bitcast.3, bf16[1,16,384]{2,1,0:T(8,128)(2,1)} %wg_any.1, bf16[1,16,384]{2,1,0:T(8,128)(2,1)} %wu_any.1, ...), custom_call_target="tpu_custom_call" | custom-call | flops 3000000000 | bytes 2000000 | tf_op jit(solution)/shard_map/pallas_call | solution.py:633
  84.9 0.8 shard_map.95
